TPU v7x, 128 devices: a whole 4x4x4 slice. The times are simulated.
128 devices in a mesh: table: 16 (over z, x), seq: 2 (over core), dp: 4 (over y).
Axes of the slice: x: 4, y: 4, z: 4, core: 2. Of those that a mesh axis runs over, the one named last changes fastest.
Arguments:
- table_wide: bfloat16 [256, 262144], P(None, ('table', 'seq', 'dp')), may hold values from -6 to 6
- table_mid: bfloat16 [128, 262144], P(None, ('table', 'seq', 'dp')), may hold values from -6 to 6
- table_narrow: bfloat16 [64, 262144], P(None, ('table', 'seq', 'dp')), may hold values from -6 to 6
- table_thin: bfloat16 [32, 262144], P(None, ('table', 'seq', 'dp')), may hold values from -6 to 6
- band_proj: bfloat16 [480, 512], replicated, may hold values from -0.5 to 0.5
- first_conv_weight: bfloat16 [1536, 512], replicated, may hold values from -0.15625 to 0.15625
- first_conv_bias: float32 [512], replicated, may hold values from -3 to 3
- gain_first: float32 [512], replicated, may hold values from 0.25 to 1.75
- offset_first: float32 [512], replicated, may hold values from -3 to 3
- second_conv_weight: bfloat16 [1536, 512], replicated, may hold values from -0.15625 to 0.15625
- second_conv_bias: float32 [512], replicated, may hold values from -3 to 3
- gain_second: float32 [512], replicated, may hold values from 0.25 to 1.75
- offset_second: float32 [512], replicated, may hold values from -3 to 3
- slot_event: int32 [64, 2, 128, 8], P(('table', 'dp'), 'seq'), may hold values from 0 to 511, as said below
- slot_counts: int32 [64, 2, 128], P(('table', 'dp'), 'seq'), may hold values from 0 to 8, as said below
- slot_band: int32 [64, 2, 128, 8], P(('table', 'dp'), 'seq'), may hold values from 0 to 3
- slot_row: int32 [64, 2, 128, 8], P(('table', 'dp'), 'seq'), may hold values from 0 to 2047
- out_grad: bfloat16 [64, 1024, 512], P(('table', 'dp'), 'seq'), may hold values from -6 to 6
Outputs:
- block_out: bfloat16 [64, 1024, 512], P(('table', 'dp'), 'seq')
- grad_table_wide: bfloat16 [256, 262144], P(None, ('table', 'seq', 'dp'))
- grad_table_mid: bfloat16 [128, 262144], P(None, ('table', 'seq', 'dp'))
- grad_table_narrow: bfloat16 [64, 262144], P(None, ('table', 'seq', 'dp'))
- grad_table_thin: bfloat16 [32, 262144], P(None, ('table', 'seq', 'dp'))
- grad_proj: float32 [480, 512], replicated
- grad_conv_first: float32 [1536, 512], replicated
- grad_conv_second: float32 [1536, 512], replicated
- grad_vectors: float32 [6, 512], replicated
Inputs may be any that keep to these rules, and one draw needn't show every extreme that they name: `slot_counts`: counts of one device's block sum to 512; one owner, the same for every device, has exactly 8 live slots from every device. `slot_event`: live slots are the first slot_counts slots toward each owner; the live slots of one device's block name each of its 512 positions exactly once; other slots hold arbitrary positions.
All inputs are finite; a program needn't handle non-finite values.
Results may differ from a plain program's by a relative error of at most 0.0085.
Values may be sent and summed in bfloat16 or wider, within the bound.
A program may use at most 128 MiB of HBM per device.

v0:
```python
import functools

import jax
import jax.numpy as jnp
from jax import lax
from jax.experimental import pallas as pl
from jax.experimental.pallas import tpu as pltpu
from jax.sharding import PartitionSpec as P

MESH = pl.DeviceIdType.MESH
F32, BF16, I32 = jnp.float32, jnp.bfloat16, jnp.int32
STEP = 4
EPS = 1e-5
NDEV, CAP, SLOTS, LEN, CH, ROWS = 128, 8, 1024, 512, 512, 2048
HALF = 256
BLK = 32
GC = 0.7978845608028654
GA = 0.044715
NT = (((1,), (1,)), ((), ()))
TN = (((0,), (0,)), ((), ()))
BASES = (0, 1536, 3072)
SPANS = (768, 768, 256)
AXES = ("x", "y", "z")


def dot(a, b, dims=None):
    if dims is None:
        return jnp.dot(a, b, preferred_element_type=F32)
    return lax.dot_general(a, b, dims, preferred_element_type=F32)


def gelu_parts(u):
    sq = u * u
    t = jnp.tanh(GC * (u + GA * u * sq))
    half = 0.5 * (1.0 + t)
    slope = half + (0.5 * GC) * u * (1.0 - t * t) * (1.0 + (3.0 * GA) * sq)
    return u * half, slope


def row_mean(v):
    return jnp.sum(v, axis=-1, keepdims=True) * (1.0 / CH)


def fold(v):
    return jnp.sum(v.reshape(v.shape[0] // 8, 8, v.shape[1]), axis=0)


def kernel(
    wide, mid, narrow, thin, proj, w1, w2, og,
    codes, target, sband, b1, g1, o1, b2, g2, o2,
    block_out, t_wide, t_mid, t_narrow, t_thin, grads,
    tcat, pext, w1v, w2v, ogv, relay, fetched, code_sc, onehot, place, msg, answers,
    eband, xm, e32, ehalo_s, ehalo_r, estack, hid, norm1, slope1, rstd1, a32, ahalo_s, ahalo_r, astack,
    bov, g2f, ghalo2_s, ghalo2_r, g1f, ghalo1_s, ghalo1_r, ge, gmsg, gotg, mt, tout,
    own_a, own_b, own_c, xs_a, xs_b, xs_c, xr_a, xr_b, xr_c, u_a, u_b, u_c,
    s1_r, s2_s, s2_r, s3_q, zbuf,
    in_sem, rq_sem, ans_sem, halo_sem, gr_sem, core_sem, ar_sem, fin_sem, out_sem, loc_sem,
):
    t, s, d = lax.axis_index("table"), lax.axis_index("seq"), lax.axis_index("dp")
    sd = s * 4 + d
    me = t * 8 + sd
    coord = {"x": lax.rem(t, 4), "y": d, "z": t // 4}
    other = 1 - s

    def peer(axis, j):
        n = lax.rem(coord[axis] + j, 4)
        if axis == "x":
            return n, (t - coord["x"] + n, s, d)
        if axis == "y":
            return n, (t, s, n)
        return n, (n * 4 + coord["x"], s, d)

    def dev(o):
        return (o // 8, lax.rem(o // 4, 2), lax.rem(o, 4))

    def rcopy(src, dst, send, recv, to):
        return pltpu.make_async_remote_copy(
            src_ref=src, dst_ref=dst, send_sem=send, recv_sem=recv, device_id=to, device_id_type=MESH
        )

    partner = (t, other, d)

    ins = [
        (wide, tcat.at[0:256]), (mid, tcat.at[256:384]), (narrow, tcat.at[384:448]),
        (thin, tcat.at[448:480]), (proj, pext.at[0:480]), (w1, w1v), (w2, w2v), (og, ogv),
    ]
    in_copies = [pltpu.make_async_copy(a, b, in_sem.at[i]) for i, (a, b) in enumerate(ins)]
    for c in in_copies:
        c.start()

    bar = pltpu.get_barrier_semaphore()

    def near(k):
        n = lax.rem(sd + k, 8)
        return n, (t, n // 4, lax.rem(n, 4))

    def far(k):
        n = lax.rem(t + k, 16)
        return n, (n, s, d)

    def sig_near(k, c):
        pl.semaphore_signal(bar, inc=1, device_id=near(k)[1], device_id_type=MESH)
        return c

    def sig_far(k, c):
        pl.semaphore_signal(bar, inc=1, device_id=far(k)[1], device_id_type=MESH)
        return c

    lax.fori_loop(1, 8, sig_near, 0)
    lax.fori_loop(1, 16, sig_far, 0)
    pl.semaphore_wait(bar, 22)

    def ask_near(k, c):
        n, to = near(k)
        rcopy(codes.at[:, n], relay.at[sd], rq_sem.at[0], rq_sem.at[1], to).start()
        return c

    lax.fori_loop(1, 8, ask_near, 0)
    own = pltpu.make_async_copy(codes.at[:, sd], relay.at[sd], loc_sem.at[0])
    own.start()

    hit = lax.broadcasted_iota(I32, (LEN, SLOTS), 0) == target[...]
    place[...] = hit.astype(F32).astype(BF16)
    ev = jnp.sum(jnp.where(hit, sband[...].astype(F32), 0.0), axis=1, keepdims=True)
    eband[...] = jnp.broadcast_to(ev, (LEN, 128))
    pext[480:512] = jnp.zeros((32, CH), BF16)
    tcat[480:512] = jnp.zeros((32, ROWS), BF16)

    own.wait()
    w = rcopy(relay.at[pl.ds(0, 7)], relay.at[pl.ds(0, 7)], rq_sem.at[0], rq_sem.at[1], partner)
    w.wait_recv()

    def ask_far(k, c):
        n, to = far(k)
        rcopy(relay.at[:, n], fetched.at[t], rq_sem.at[2], rq_sem.at[3], to).start()
        return c

    lax.fori_loop(1, 16, ask_far, 0)
    own = pltpu.make_async_copy(relay.at[:, t], fetched.at[t], loc_sem.at[0])
    own.start()
    own.wait()
    w2nd = rcopy(fetched.at[pl.ds(0, 15)], fetched.at[pl.ds(0, 15)], rq_sem.at[2], rq_sem.at[3], partner)
    w2nd.wait_recv()

    got = fetched[...].reshape(NDEV, 1, 128).astype(F32)
    wide_got = jnp.broadcast_to(got, (NDEV, CAP, 128))
    lane = lax.broadcasted_iota(I32, (NDEV, CAP, 128), 2)
    sub = lax.broadcasted_iota(I32, (NDEV, CAP, 128), 1)
    picked = jnp.sum(jnp.where(lane == sub, wide_got, 0.0), axis=-1, keepdims=True)
    code_sc[...] = jnp.broadcast_to(picked, (NDEV, CAP, 128)).reshape(SLOTS, 128).astype(I32)

    for c in in_copies[:4]:
        c.wait()

    lane128 = lax.broadcasted_iota(I32, (HALF, 128), 1)

    def lookup(i, carry):
        cb = lax.rem(me // 32 + i, 4)
        rows = pl.ds(pl.multiple_of(cb * HALF, HALF), HALF)
        code = code_sc[rows]
        row, band = code & (ROWS - 1), code >> 11
        for b in range(ROWS // 128):
            onehot[rows, b * 128 : (b + 1) * 128] = (row == lane128 + b * 128).astype(F32).astype(BF16)
        got_rows = dot(onehot[rows], tcat[...], NT)
        first = jnp.where(
            band == 0, got_rows[:, 0:128], jnp.where(band == 1, got_rows[:, 256:384], got_rows[:, 384:512])
        )
        both = jnp.concatenate(
            [first.reshape(32, 8, 128), got_rows[:, 128:256].reshape(32, 8, 128)], axis=1
        )
        msg[pl.ds(cb * 32, 32)] = both.astype(BF16)

        def send(k, c):
            to = cb * 32 + lax.rem(me + k, 32)

            @pl.when(to != me)
            def _():
                rcopy(msg.at[to], answers.at[me], ans_sem.at[0], ans_sem.at[1], dev(to)).start()

            return c

        return lax.fori_loop(0, 32, send, carry)

    lax.fori_loop(0, 4, lookup, 0)
    own = pltpu.make_async_copy(msg.at[me], answers.at[me], loc_sem.at[0])
    own.start()
    own.wait()
    wa = rcopy(msg.at[pl.ds(0, 127)], answers.at[pl.ds(0, 127)], ans_sem.at[0], ans_sem.at[1], partner)
    wa.wait_recv()
    in_copies[4].wait()

    halves = answers[...].astype(F32)
    flat = jnp.concatenate(
        [halves[:, 0:8].reshape(SLOTS, 128), halves[:, 8:16].reshape(SLOTS, 128)], axis=1
    ).astype(BF16)
    lane_e = lax.broadcasted_iota(I32, (LEN, 128), 1)
    x = dot(place[...], flat)
    eb = eband[...]
    tail = ((eb == 2.0) & (lane_e < 64)) | ((eb == 3.0) & (lane_e >= 64) & (lane_e < 96))
    xm[:, 0:128] = jnp.where(eb == 0.0, x[:, 0:128], 0.0).astype(BF16)
    xm[:, 128:256] = jnp.where(eb == 0.0, x[:, 128:256], 0.0).astype(BF16)
    xm[:, 256:384] = jnp.where(eb == 1.0, x[:, 0:128], 0.0).astype(BF16)
    xm[:, 384:512] = jnp.where(tail, x[:, 0:128], 0.0).astype(BF16)

    def halo(i, src, dst):
        return rcopy(src, dst, halo_sem.at[2 * i], halo_sem.at[2 * i + 1], partner)

    hi, lo = slice(HALF, LEN), slice(0, HALF)
    e_hi = dot(xm[hi], pext[...]).astype(BF16)
    ehalo_s[...] = e_hi[HALF - 16 :]
    h_e = halo(0, ehalo_s, ehalo_r)
    h_e.start()
    e32[8 + HALF :] = e_hi.astype(F32)
    e_lo = dot(xm[lo], pext[...]).astype(BF16)
    e32[8 : 8 + HALF] = e_lo.astype(F32)

    def stack(part, src, dst, gap):
        base = 0 if part == "lo" else HALF
        for k in range(3):
            dst[base : base + HALF, k * CH : (k + 1) * CH] = src[
                base + (2 - k) * gap : base + (2 - k) * gap + HALF
            ].astype(BF16)

    first_core = s == 0

    def layer1(base):
        hid[...] = dot(estack[base : base + HALF], w1v[...]) + b1[...]

        def block(i, c):
            r0 = pl.multiple_of(i * BLK, BLK)
            h = hid[pl.ds(r0, BLK)]
            cen = h - row_mean(h)
            rs = lax.rsqrt(row_mean(cen * cen) + EPS)
            n = cen * rs
            act, slope = gelu_parts(n * g1[...] + o1[...])
            at = pl.ds(base + r0, BLK)
            norm1[at] = n
            slope1[at] = slope
            rstd1[at] = jnp.broadcast_to(rs, (BLK, 128))
            a32[pl.ds(base + r0 + 16, BLK)] = act.astype(BF16).astype(F32)
            return c

        lax.fori_loop(0, HALF // BLK, block, 0)

    in_copies[5].wait()
    stack("hi", e32, estack, STEP)
    layer1(HALF)
    ahalo_s[...] = a32[LEN:].astype(BF16)
    h_a = halo(1, ahalo_s, ahalo_r)
    h_a.start()
    h_e.wait_recv()
    e32[0:8] = jnp.where(first_core, 0.0, ehalo_r[...].astype(F32)[8:16])
    stack("lo", e32, estack, STEP)
    layer1(0)

    in_copies[6].wait()
    in_copies[7].wait()
    zero8 = jnp.zeros((8, CH), F32)

    def layer2(base, sums):
        hid[...] = dot(astack[base : base + HALF], w2v[...]) + b2[...]

        def block(i, c):
            r0 = pl.multiple_of(i * BLK, BLK)
            h = hid[pl.ds(r0, BLK)]
            cen = h - row_mean(h)
            rs = lax.rsqrt(row_mean(cen * cen) + EPS)
            n = cen * rs
            act, slope = gelu_parts(n * g2[...] + o2[...])
            at = pl.ds(base + r0, BLK)
            bov[at] = (e32[pl.ds(base + r0 + 8, BLK)] + act).astype(BF16)
            du = ogv[at].astype(F32) * slope
            dn = du * g2[...]
            dh = (rs * (dn - row_mean(dn) - n * row_mean(dn * n))).astype(BF16).astype(F32)
            g2f[at] = dh
            return (c[0] + fold(dh), c[1] + fold(du * n), c[2] + fold(du))

        return lax.fori_loop(0, HALF // BLK, block, sums)

    stack("hi", a32, astack, 2 * STEP)
    sums2 = layer2(HALF, (zero8, zero8, zero8))
    h_a.wait_recv()
    a32[0:16] = jnp.where(first_core, 0.0, ahalo_r[...].astype(F32))
    stack("lo", a32, astack, 2 * STEP)
    sums2 = layer2(0, sums2)
    ghalo2_s[...] = g2f[0:16].astype(BF16)
    h_g2 = halo(2, ghalo2_s, ghalo2_r)
    h_g2.start()
    out_bo = pltpu.make_async_copy(bov, block_out, out_sem.at[0])
    out_bo.start()

    owns, xss, xrs, us = (own_a, own_b, own_c), (xs_a, xs_b, xs_c), (xr_a, xr_b, xr_c), (u_a, u_b, u_c)

    def core_copy(g):
        return rcopy(xss[g], xrs[g], core_sem.at[2 * g], core_sem.at[2 * g + 1], partner)

    def parts_of(g):
        return (3 * g, 3 * g + 1, 3 * g + 2) if g < 2 else (6,)

    def order(p):
        k = p % 3
        return AXES[k], AXES[(k + 1) % 3], AXES[(k + 2) % 3]

    def sems(p, stage):
        return ar_sem.at[p * 10 + 2 * stage], ar_sem.at[p * 10 + 2 * stage + 1]

    def home(p):
        g = min(p // 3, 2)
        return pl.multiple_of(BASES[g] + s * SPANS[g] + (p - 3 * g) * 256, 256)

    def wait3(p, stage, ref):
        send, recv = sems(p, stage)
        rcopy(ref, ref, send, recv, partner).wait_recv()

    def wait3_send(p, stage, ref):
        send, recv = sems(p, stage)
        rcopy(ref, ref, send, recv, partner).wait_send()

    def ar_stage0(g):
        core_copy(g).wait_recv()
        us[g][...] = (owns[g][...] + xrs[g][...].astype(F32)).astype(BF16)
        for p in parts_of(g):
            a = order(p)[0]
            send, recv = sems(p, 0)
            for j in (1, 2, 3):
                n, to = peer(a, j)
                off = pl.multiple_of((p - 3 * g) * 256 + n * 64, 64)
                rcopy(us[g].at[pl.ds(off, 64)], s1_r.at[p, j - 1], send, recv, to).start()

    def ar_stage1(g):
        for p in parts_of(g):
            a, b, _ = order(p)
            wait3(p, 0, s1_r.at[p])
            off = pl.multiple_of((p - 3 * g) * 256 + coord[a] * 64, 64)
            v = us[g][pl.ds(off, 64)].astype(F32)
            for j in range(3):
                v = v + s1_r[p, j].astype(F32)
            s2_s[p] = v.astype(BF16)
            send, recv = sems(p, 1)
            for j in (1, 2, 3):
                n, to = peer(b, j)
                rcopy(
                    s2_s.at[p, pl.ds(pl.multiple_of(n * 16, 16), 16)], s2_r.at[p, j - 1], send, recv, to
                ).start()

    def ar_stage2(g):
        for p in parts_of(g):
            _, b, c = order(p)
            wait3(p, 1, s2_r.at[p])
            v = s2_s[p, pl.ds(pl.multiple_of(coord[b] * 16, 16), 16)].astype(F32)
            for j in range(3):
                v = v + s2_r[p, j].astype(F32)
            s3_q[p, coord[c]] = v.astype(BF16)
            send, recv = sems(p, 2)
            for j in (1, 2, 3):
                _, to = peer(c, j)
                rcopy(s3_q.at[p, coord[c]], s3_q.at[p, coord[c]], send, recv, to).start()

    def ar_stage3(g):
        for p in parts_of(g):
            a, b, c = order(p)
            wait3(p, 2, s3_q.at[p, pl.ds(0, 3)])
            q = s3_q[p].astype(F32)
            at = pl.ds(pl.multiple_of(home(p) + coord[a] * 64 + coord[b] * 16, 16), 16)
            zbuf[at] = (((q[0] + q[1]) + q[2]) + q[3]).astype(BF16)
            send, recv = sems(p, 3)
            for j in (1, 2, 3):
                _, to = peer(b, j)
                rcopy(zbuf.at[at], zbuf.at[at], send, recv, to).start()

    def ar_stage4(g):
        for p in parts_of(g):
            a, b, c = order(p)
            wait3(p, 3, zbuf.at[pl.ds(0, 48)])
            at = pl.ds(pl.multiple_of(home(p) + coord[a] * 64, 64), 64)
            send, recv = sems(p, 4)
            for j in (1, 2, 3):
                _, to = peer(a, j)
                rcopy(zbuf.at[at], zbuf.at[at], send, recv, to).start()

    def ar_stage5(g):
        for p in parts_of(g):
            wait3(p, 4, zbuf.at[pl.ds(0, 192)])
            at = pl.ds(home(p), 256)
            rcopy(zbuf.at[at], zbuf.at[at], fin_sem.at[2 * p], fin_sem.at[2 * p + 1], partner).start()

    def ar_finish(g):
        for p in parts_of(g):
            at = pl.ds(home(p), 256)
            rcopy(zbuf.at[at], zbuf.at[at], fin_sem.at[2 * p], fin_sem.at[2 * p + 1], partner).wait()

    def ar_drain(g):
        core_copy(g).wait_send()
        for p in parts_of(g):
            wait3_send(p, 0, s1_r.at[p])
            wait3_send(p, 1, s2_r.at[p])
            wait3_send(p, 2, s3_q.at[p, pl.ds(0, 3)])
            wait3_send(p, 3, zbuf.at[pl.ds(0, 48)])
            wait3_send(p, 4, zbuf.at[pl.ds(0, 192)])

    def weight_sum(g, taps, gb):
        theirs = pl.ds(pl.multiple_of(other * 768, 256), 768)
        mine = pl.ds(pl.multiple_of(s * 768, 256), 768)
        xss[g][...] = dot(taps[:, theirs], gb, TN).astype(BF16)
        core_copy(g).start()
        owns[g][...] = dot(taps[:, mine], gb, TN)

    weight_sum(0, astack, g2f[0:LEN].astype(BF16))

    def back1(base, sums):
        hid[...] = sum(
            dot(g2f[base + k * 8 : base + k * 8 + HALF].astype(BF16), w2v[k * CH : (k + 1) * CH], NT)
            for k in range(3)
        )

        def block(i, c):
            r0 = pl.multiple_of(i * BLK, BLK)
            at = pl.ds(base + r0, BLK)
            n = norm1[at]
            du = hid[pl.ds(r0, BLK)] * slope1[at]
            dn = du * g1[...]
            rs = rstd1[at][:, 0:1]
            dh = (rs * (dn - row_mean(dn) - n * row_mean(dn * n))).astype(BF16).astype(F32)
            g1f[at] = dh
            return (c[0] + fold(dh), c[1] + fold(du * n), c[2] + fold(du))

        return lax.fori_loop(0, HALF // BLK, block, sums)

    sums1 = back1(0, (zero8, zero8, zero8))
    ghalo1_s[...] = g1f[0:16].astype(BF16)
    h_g1 = halo(3, ghalo1_s, ghalo1_r)
    h_g1.start()
    ar_stage0(0)
    h_g2.wait_recv()
    g2f[LEN:] = jnp.where(first_core, ghalo2_r[...].astype(F32), 0.0)
    sums1 = back1(HALF, sums1)
    ar_stage1(0)
    weight_sum(1, estack, g1f[0:LEN].astype(BF16))
    h_g1.wait_recv()
    g1f[LEN:] = jnp.where(first_core, ghalo1_r[...].astype(F32)[0:8], 0.0)
    ar_stage2(0)

    for base in (0, HALF):
        ge[base : base + HALF] = (
            ogv[base : base + HALF].astype(F32)
            + sum(
                dot(g1f[base + k * 4 : base + k * 4 + HALF].astype(BF16), w1v[k * CH : (k + 1) * CH], NT)
                for k in range(3)
            )
        ).astype(BF16)
    rg = dot(ge[...], pext[...], NT)
    first = jnp.where(eb == 0.0, rg[:, 0:128], jnp.where(eb == 1.0, rg[:, 256:384], rg[:, 384:512]))
    rgb = jnp.concatenate([first, rg[:, 128:256]], axis=1).astype(BF16)
    slots = dot(place[...], rgb, TN)
    gmsg[...] = jnp.concatenate(
        [slots[:, 0:128].reshape(NDEV, 8, 128), slots[:, 128:256].reshape(NDEV, 8, 128)], axis=1
    ).astype(BF16)

    def send_grad(k, c):
        to = lax.rem(me + k, NDEV)
        rcopy(gmsg.at[to], gotg.at[me], gr_sem.at[0], gr_sem.at[1], dev(to)).start()
        return c

    ar_stage0(1)
    lax.fori_loop(1, NDEV, send_grad, 0)
    own = pltpu.make_async_copy(gmsg.at[me], gotg.at[me], loc_sem.at[0])
    own.start()

    pg = dot(xm[...], ge[...], TN)
    owns_full = hid
    vec = jnp.concatenate(
        [jnp.sum(v, axis=0, keepdims=True) for v in (*sums1, *sums2)] + [jnp.zeros((2, CH), F32)], axis=0
    )
    own_c[...] = pg
    own_c[480:488] = vec
    xs_c[...] = own_c[pl.ds(pl.multiple_of(other * 256, 256), 256)].astype(BF16)
    core_copy(2).start()
    ar_stage3(0)
    ar_stage1(1)

    core_copy(2).wait_recv()
    u_c[...] = (own_c[pl.ds(pl.multiple_of(s * 256, 256), 256)] + xr_c[...].astype(F32)).astype(BF16)
    a6 = order(6)[0]
    for j in (1, 2, 3):
        n, to = peer(a6, j)
        send, recv = sems(6, 0)
        rcopy(u_c.at[pl.ds(pl.multiple_of(n * 64, 64), 64)], s1_r.at[6, j - 1], send, recv, to).start()
    ar_stage4(0)
    ar_stage2(1)
    ar_stage1(2)
    ar_stage5(0)
    ar_stage3(1)
    ar_stage2(2)
    ar_stage4(1)
    ar_stage3(2)

    own.wait()
    wg = rcopy(gmsg.at[pl.ds(0, 127)], gotg.at[pl.ds(0, 127)], gr_sem.at[0], gr_sem.at[1], partner)
    wg.wait_recv()
    band = code_sc[...] >> 11
    lane_s = lax.broadcasted_iota(I32, (SLOTS, 128), 1)
    both = gotg[...].astype(F32)
    h0, h1 = both[:, 0:8].reshape(SLOTS, 128), both[:, 8:16].reshape(SLOTS, 128)
    tail = ((band == 2) & (lane_s < 64)) | ((band == 3) & (lane_s >= 64) & (lane_s < 96))
    mt[0:128] = jnp.where(band == 0, h0, 0.0).T.astype(BF16)
    mt[128:256] = jnp.where(band == 0, h1, 0.0).T.astype(BF16)
    mt[256:384] = jnp.where(band == 1, h0, 0.0).T.astype(BF16)
    mt[384:512] = jnp.where(tail, h0, 0.0).T.astype(BF16)
    for b in range(4):
        tout[:, b * 512 : (b + 1) * 512] = dot(mt[...], onehot[:, b * 512 : (b + 1) * 512]).astype(BF16)
    outs = [
        (tout.at[0:256], t_wide), (tout.at[256:384], t_mid),
        (tout.at[384:448], t_narrow), (tout.at[448:480], t_thin),
    ]
    out_copies = [pltpu.make_async_copy(a, b, out_sem.at[1 + i]) for i, (a, b) in enumerate(outs)]
    for c in out_copies:
        c.start()

    ar_stage5(1)
    ar_stage4(2)
    ar_stage5(2)
    for g in range(3):
        ar_finish(g)
    out_z = pltpu.make_async_copy(zbuf, grads, out_sem.at[5])
    out_z.start()
    for g in range(3):
        ar_drain(g)
    rcopy(relay.at[pl.ds(0, 7)], relay.at[pl.ds(0, 7)], rq_sem.at[0], rq_sem.at[1], partner).wait_send()
    w2nd.wait_send()
    wa.wait_send()
    wg.wait_send()
    for h in (h_e, h_a, h_g2, h_g1):
        h.wait_send()
    out_bo.wait()
    for c in out_copies:
        c.wait()
    out_z.wait()


def scratch():
    v = pltpu.VMEM
    dma = pltpu.SemaphoreType.DMA
    return [
        v((512, ROWS), BF16), v((512, CH), BF16), v((1536, CH), BF16), v((1536, CH), BF16), v((LEN, CH), BF16),
        v((8, 16, 1, 128), I32), v((16, 8, 1, 128), I32), v((SLOTS, 128), I32), v((SLOTS, ROWS), BF16),
        v((LEN, SLOTS), BF16), v((NDEV, 16, 128), BF16), v((NDEV, 16, 128), BF16),
        v((LEN, 128), F32), v((LEN, 512), BF16), v((8 + LEN, CH), F32), v((16, CH), BF16), v((16, CH), BF16),
        v((LEN, 1536), BF16), v((HALF, CH), F32), v((LEN, CH), F32), v((LEN, CH), F32), v((LEN, 128), F32),
        v((16 + LEN, CH), F32), v((16, CH), BF16), v((16, CH), BF16), v((LEN, 1536), BF16),
        v((LEN, CH), BF16), v((LEN + 16, CH), F32), v((16, CH), BF16), v((16, CH), BF16),
        v((LEN + 8, CH), F32), v((16, CH), BF16), v((16, CH), BF16), v((LEN, CH), BF16),
        v((NDEV, 16, 128), BF16), v((NDEV, 16, 128), BF16), v((512, SLOTS), BF16), v((512, ROWS), BF16),
        v((768, CH), F32), v((768, CH), F32), v((512, CH), F32),
        v((768, CH), BF16), v((768, CH), BF16), v((256, CH), BF16),
        v((768, CH), BF16), v((768, CH), BF16), v((256, CH), BF16),
        v((768, CH), BF16), v((768, CH), BF16), v((256, CH), BF16),
        v((7, 3, 64, CH), BF16), v((7, 64, CH), BF16), v((7, 3, 16, CH), BF16), v((7, 4, 16, CH), BF16),
        v((3584, CH), BF16),
        dma((8,)), dma((4,)), dma((2,)), dma((8,)), dma((2,)), dma((6,)), dma((70,)), dma((14,)), dma((6,)), dma((1,)),
    ]


def shards(
    table_wide, table_mid, table_narrow, table_thin, band_proj, first_conv_weight, first_conv_bias,
    gain_first, offset_first, second_conv_weight, second_conv_bias, gain_second, offset_second,
    slot_event, slot_counts, slot_band, slot_row, out_grad,
):
    live = jnp.arange(CAP, dtype=I32)[None, :] < slot_counts[0, 0][:, None]
    code = slot_row[0, 0] + ROWS * slot_band[0, 0]
    codes = jnp.pad(code, ((0, 0), (0, 128 - CAP))).reshape(16, 8, 1, 128)
    target = jnp.where(live, slot_event[0, 0], LEN).reshape(1, SLOTS)
    sband = slot_band[0, 0].reshape(1, SLOTS)
    vecs = [
        v.reshape(1, CH)
        for v in (first_conv_bias, gain_first, offset_first, second_conv_bias, gain_second, offset_second)
    ]
    hbm, vmem = pl.BlockSpec(memory_space=pl.ANY), pl.BlockSpec(memory_space=pltpu.VMEM)
    sds = jax.ShapeDtypeStruct
    block_out, tw, tm, tn, tt, grads = pl.pallas_call(
        kernel,
        out_shape=[
            sds((LEN, CH), BF16), sds((256, ROWS), BF16), sds((128, ROWS), BF16), sds((64, ROWS), BF16),
            sds((32, ROWS), BF16), sds((3584, CH), BF16),
        ],
        in_specs=[hbm] * 8 + [vmem] * 9,
        out_specs=[hbm] * 6,
        scratch_shapes=scratch(),
        compiler_params=pltpu.CompilerParams(
            collective_id=0, has_side_effects=True, vmem_limit_bytes=60 << 20
        ),
        cost_estimate=pl.CostEstimate(flops=12 * 10**9, bytes_accessed=14 * 2**20, transcendentals=2**19),
    )(
        table_wide, table_mid, table_narrow, table_thin, band_proj, first_conv_weight, second_conv_weight,
        out_grad[0], codes, target, sband, *vecs,
    )
    scale = 1.0 / float(NDEV * LEN) ** 0.5
    wide_grads = grads.astype(F32) * scale
    return (
        block_out[None], tw, tm, tn, tt, wide_grads[3072:3552], wide_grads[1536:3072], wide_grads[0:1536],
        wide_grads[3552:3558],
    )


def solution(mesh):
    rows = P(None, ("table", "seq", "dp"))
    hist = ("table", "dp")
    in_specs = (rows,) * 4 + (P(),) * 9 + (
        P(hist, "seq", None, None), P(hist, "seq", None), P(hist, "seq", None, None), P(hist, "seq", None, None),
        P(hist, "seq", None),
    )
    out_specs = (P(hist, "seq", None),) + (rows,) * 4 + (P(),) * 4
    return jax.shard_map(shards, mesh=mesh, in_specs=in_specs, out_specs=out_specs, check_vma=False)
```

profile of v0, /device:TPU:1, one launch (start us, length us, event | category | flops | bytes accessed | tf_op | source)
XLA Modules:
  0.0 111.5 jit_solution(17517901577300769977)
XLA Ops:
  0.6 0.7 add_bitcast_fusion
  1.3 0.1 copy.33
  1.5 0.6 pad.4.clone
  2.1 0.7 iota_compare_fusion
  2.8 0.1 lt.29
  2.9 0.8 copy.31
  3.7 0.1 squeeze.9
  3.8 0.6 broadcast_select_fusion.target
  4.4 0.8 copy.32
  5.2 0.7 reshape_squeeze.3.sband
  5.9 93.6 %shard_map.241 = (bf16[512,512]{1,0:T(8,128)(2,1)}, bf16[256,2048]{1,0:T(8,128)(2,1)}, bf16[128,2048]{1,0:T(8,128)(2,1)}, bf16[64,2048]{1,0:T(8,128)(2,1)}, bf16...) custom-call(bf16[256,2048]{1,0:T(8,128)(2,1)} %wide.1, bf16[128,2048]{1,0:T(8,128)(2,1)} %mid.1, bf16[64,2048]{1,0:T(8,128)(2,1)} %narrow.1, ...), custom_call_target="tpu_custom_call" | custom-call | flops 12000000000 | bytes 14680064 | tf_op jit(solution)/shard_map/pallas_call | solution.py:579
  99.5 3.1 %convert_multiply_fusion = f32[3584,512]{1,0:T(8,128)S(1)} fusion(bf16[3584,512]{1,0:T(8,128)(2,1)} %get-tuple-element.20), kind=kLoop, calls=%fused_computation | loop fusion | flops 3670016 | bytes 11010048 | tf_op jit(solution)/shard_map/mul | solution.py:597
  102.6 1.0 slice.16
  103.6 0.0 copy-start.2
  103.6 0.0 copy-start
  103.6 0.0 copy-start.1
  103.6 3.4 %fusion = (f32[1536,512]{1,0:T(8,128)}, f32[1536,512]{1,0:T(8,128)}) fusion(f32[3584,512]{1,0:T(8,128)S(1)} %convert_multiply_fusion), kind=kLoop, calls=%fused_computation.4 | loop fusion | bytes 12582912 | tf_op jit(solution)/shard_map/slice | solution.py:599
  107.0 0.0 copy-start.3
  107.0 0.0 copy-start.4
  107.0 0.6 slice.19
  107.6 0.0 copy-done.2
  107.6 0.8 copy.39
  108.4 0.0 copy-done
  108.4 1.0 copy.40
  109.4 0.0 copy-done.1
  109.4 0.8 copy.41
  110.2 0.0 copy-done.3
  110.2 0.7 copy.42
  110.9 0.0 copy-done.4
  110.9 0.7 copy.43
Async XLA Ops:
  103.6 4.0 %copy-start.2 = (bf16[512,512]{1,0:T(8,128)(2,1)S(1)}, bf16[512,512]{1,0:T(8,128)(2,1)}, u32[]{:S(2)}) copy-start(bf16[512,512]{1,0:T(8,128)(2,1)} %get-tuple-element.15) | copy-start | bytes 1572868
  103.6 4.8 %copy-start = (bf16[256,2048]{1,0:T(8,128)(2,1)S(1)}, bf16[256,2048]{1,0:T(8,128)(2,1)}, u32[]{:S(2)}) copy-start(bf16[256,2048]{1,0:T(8,128)(2,1)} %get-tuple-element.33) | copy-start | bytes 3145732
  103.6 5.8 %copy-start.1 = (bf16[128,2048]{1,0:T(8,128)(2,1)S(1)}, bf16[128,2048]{1,0:T(8,128)(2,1)}, u32[]{:S(2)}) copy-start(bf16[128,2048]{1,0:T(8,128)(2,1)} %get-tuple-element.34) | copy-start | bytes 1572868
  107.0 3.2 %copy-start.3 = (bf16[64,2048]{1,0:T(8,128)(2,1)S(1)}, bf16[64,2048]{1,0:T(8,128)(2,1)}, u32[]{:S(2)}) copy-start(bf16[64,2048]{1,0:T(8,128)(2,1)} %get-tuple-element.35) | copy-start | bytes 786436
  107.0 3.9 %copy-start.4 = (bf16[32,2048]{1,0:T(8,128)(2,1)S(1)}, bf16[32,2048]{1,0:T(8,128)(2,1)}, u32[]{:S(2)}) copy-start(bf16[32,2048]{1,0:T(8,128)(2,1)} %get-tuple-element.36) | copy-start | bytes 393220
where the time goes:
time: 112 us
  Pallas kernels  93.6 us (84%)
  local copies, waits for them, and re-layouts  12.2 us (11%)
  other arithmetic  5.12 us (5%)
    pallas_call x1, Pallas kernels, shards(): pl.pallas_call(kernel, out_shape=[sds((LEN, CH), BF16), sds((256, ROWS),...  93.6 us
    unnamed x18, local copies, waits for them, and re-layouts  5.61 us
    slice x1, local copies, waits for them, and re-layouts, shards(): wide_grads[0:1536]  3.41 us
    mul x1, other arithmetic, shards(): wide_grads = grads.astype(F32) * scale  3.08 us

commit v1 on v0

--- a/solution.py
+++ b/solution.py
@@ -1,5 +1,3 @@
-import functools
-
 import jax
 import jax.numpy as jnp
 from jax import lax
@@ -13,7 +11,7 @@
 EPS = 1e-5
 NDEV, CAP, SLOTS, LEN, CH, ROWS = 128, 8, 1024, 512, 512, 2048
 HALF = 256
-BLK = 32
+BLK = 128
 GC = 0.7978845608028654
 GA = 0.044715
 NT = (((1,), (1,)), ((), ()))
@@ -45,15 +43,33 @@
     return jnp.sum(v.reshape(v.shape[0] // 8, 8, v.shape[1]), axis=0)
 
 
+def picked_lane(v, by_row):
+    lane = lax.broadcasted_iota(I32, (NDEV, CAP, 128), 2)
+    want = lax.broadcasted_iota(I32, (NDEV, CAP, 128), 1 if by_row else 0)
+    if not by_row:
+        want = want % 8
+    one = jnp.sum(jnp.where(lane == want, v, 0.0), axis=-1, keepdims=True)
+    return jnp.broadcast_to(one, (NDEV, CAP, 128)).reshape(SLOTS, 128)
+
+
+def spread(v):
+    return picked_lane(jnp.broadcast_to(v, (NDEV, CAP, 128)), 1)
+
+
+def turned(v):
+    full = jnp.concatenate([v, jnp.zeros((120, 128), F32)], axis=0)
+    return full.T
+
+
 def kernel(
     wide, mid, narrow, thin, proj, w1, w2, og,
-    codes, target, sband, b1, g1, o1, b2, g2, o2,
+    srow, sbandr, sevent, scount, b1, g1, o1, b2, g2, o2,
     block_out, t_wide, t_mid, t_narrow, t_thin, grads,
-    tcat, pext, w1v, w2v, ogv, relay, fetched, code_sc, onehot, place, msg, answers,
+    tcat, pext, w1v, w2v, ogv, codes, relay, passed, fetched, code_sc, onehot, place, xin, msg, answers,
     eband, xm, e32, ehalo_s, ehalo_r, estack, hid, norm1, slope1, rstd1, a32, ahalo_s, ahalo_r, astack,
     bov, g2f, ghalo2_s, ghalo2_r, g1f, ghalo1_s, ghalo1_r, ge, gmsg, gotg, mt, tout,
     own_a, own_b, own_c, xs_a, xs_b, xs_c, xr_a, xr_b, xr_c, u_a, u_b, u_c,
-    s1_r, s2_s, s2_r, s3_q, zbuf,
+    s1_r, s2_s, s2_r, s3_q, c1_r, c2_s, c2_r, c3_q, zbuf,
     in_sem, rq_sem, ans_sem, halo_sem, gr_sem, core_sem, ar_sem, fin_sem, out_sem, loc_sem,
 ):
     t, s, d = lax.axis_index("table"), lax.axis_index("seq"), lax.axis_index("dp")
@@ -88,6 +104,18 @@
     for c in in_copies:
         c.start()
 
+    code_t = turned((srow[...] + ROWS * sbandr[...]).astype(F32)).reshape(16, 8, 128)
+    asked = code_t[0]
+    for k in range(1, 16):
+        asked = asked + pltpu.roll(code_t[k], k * 8, 1)
+    codes[...] = asked.astype(I32).reshape(8, 1, 128)
+
+    pending = list(c.wait for c in in_copies)
+
+    def finish():
+        for f in pending:
+            f()
+
     bar = pltpu.get_barrier_semaphore()
 
     def near(k):
@@ -112,45 +140,37 @@
 
     def ask_near(k, c):
         n, to = near(k)
-        rcopy(codes.at[:, n], relay.at[sd], rq_sem.at[0], rq_sem.at[1], to).start()
+        rcopy(codes.at[n], relay.at[sd], rq_sem.at[0], rq_sem.at[1], to).start()
         return c
 
     lax.fori_loop(1, 8, ask_near, 0)
-    own = pltpu.make_async_copy(codes.at[:, sd], relay.at[sd], loc_sem.at[0])
-    own.start()
-
-    hit = lax.broadcasted_iota(I32, (LEN, SLOTS), 0) == target[...]
-    place[...] = hit.astype(F32).astype(BF16)
-    ev = jnp.sum(jnp.where(hit, sband[...].astype(F32), 0.0), axis=1, keepdims=True)
-    eband[...] = jnp.broadcast_to(ev, (LEN, 128))
+    relay[sd] = codes[sd]
     pext[480:512] = jnp.zeros((32, CH), BF16)
     tcat[480:512] = jnp.zeros((32, ROWS), BF16)
 
-    own.wait()
     w = rcopy(relay.at[pl.ds(0, 7)], relay.at[pl.ds(0, 7)], rq_sem.at[0], rq_sem.at[1], partner)
     w.wait_recv()
+    pending.append(w.wait_send)
+
+    passed[...] = turned(relay[...].reshape(8, 128).astype(F32)).astype(I32).reshape(16, 8, 128)
 
     def ask_far(k, c):
         n, to = far(k)
-        rcopy(relay.at[:, n], fetched.at[t], rq_sem.at[2], rq_sem.at[3], to).start()
+        rcopy(passed.at[n], fetched.at[t], rq_sem.at[2], rq_sem.at[3], to).start()
         return c
 
     lax.fori_loop(1, 16, ask_far, 0)
-    own = pltpu.make_async_copy(relay.at[:, t], fetched.at[t], loc_sem.at[0])
-    own.start()
-    own.wait()
+    fetched[t] = passed[t]
     w2nd = rcopy(fetched.at[pl.ds(0, 15)], fetched.at[pl.ds(0, 15)], rq_sem.at[2], rq_sem.at[3], partner)
     w2nd.wait_recv()
-
-    got = fetched[...].reshape(NDEV, 1, 128).astype(F32)
-    wide_got = jnp.broadcast_to(got, (NDEV, CAP, 128))
-    lane = lax.broadcasted_iota(I32, (NDEV, CAP, 128), 2)
-    sub = lax.broadcasted_iota(I32, (NDEV, CAP, 128), 1)
-    picked = jnp.sum(jnp.where(lane == sub, wide_got, 0.0), axis=-1, keepdims=True)
-    code_sc[...] = jnp.broadcast_to(picked, (NDEV, CAP, 128)).reshape(SLOTS, 128).astype(I32)
+    pending.append(w2nd.wait_send)
+
+    wide_f = jnp.broadcast_to(fetched[...].astype(F32).reshape(16, 1, 8, 128), (16, 8, 8, 128))
+    code_sc[...] = picked_lane(wide_f.reshape(NDEV, CAP, 128), 0).astype(I32)
 
     for c in in_copies[:4]:
         c.wait()
+    del pending[:4]
 
     lane128 = lax.broadcasted_iota(I32, (HALF, 128), 1)
 
@@ -182,20 +202,29 @@
         return lax.fori_loop(0, 32, send, carry)
 
     lax.fori_loop(0, 4, lookup, 0)
+
+    live = lax.broadcasted_iota(I32, (CAP, NDEV), 0) < scount[...]
+    target = spread(turned(jnp.where(live, sevent[...], LEN).astype(F32)).reshape(NDEV, 1, 128)).astype(I32)
+    lane_p = lax.broadcasted_iota(I32, (SLOTS, 128), 1)
+    for b in range(4):
+        place[:, b * 128 : (b + 1) * 128] = (target == lane_p + b * 128).astype(F32).astype(BF16)
+    xin[:, 256:384] = spread(turned(sbandr[...].astype(F32)).reshape(NDEV, 1, 128)).astype(BF16)
     own = pltpu.make_async_copy(msg.at[me], answers.at[me], loc_sem.at[0])
     own.start()
     own.wait()
     wa = rcopy(msg.at[pl.ds(0, 127)], answers.at[pl.ds(0, 127)], ans_sem.at[0], ans_sem.at[1], partner)
     wa.wait_recv()
+    pending.append(wa.wait_send)
     in_copies[4].wait()
+    del pending[0]
 
     halves = answers[...].astype(F32)
-    flat = jnp.concatenate(
-        [halves[:, 0:8].reshape(SLOTS, 128), halves[:, 8:16].reshape(SLOTS, 128)], axis=1
-    ).astype(BF16)
+    xin[:, 0:128] = halves[:, 0:8].reshape(SLOTS, 128).astype(BF16)
+    xin[:, 128:256] = halves[:, 8:16].reshape(SLOTS, 128).astype(BF16)
     lane_e = lax.broadcasted_iota(I32, (LEN, 128), 1)
-    x = dot(place[...], flat)
-    eb = eband[...]
+    x = dot(place[...], xin[...], TN)
+    eb = x[:, 256:384]
+    eband[...] = eb
     tail = ((eb == 2.0) & (lane_e < 64)) | ((eb == 3.0) & (lane_e >= 64) & (lane_e < 96))
     xm[:, 0:128] = jnp.where(eb == 0.0, x[:, 0:128], 0.0).astype(BF16)
     xm[:, 128:256] = jnp.where(eb == 0.0, x[:, 128:256], 0.0).astype(BF16)
@@ -242,7 +271,9 @@
 
         lax.fori_loop(0, HALF // BLK, block, 0)
 
+    pending.append(h_e.wait_send)
     in_copies[5].wait()
+    del pending[0]
     stack("hi", e32, estack, STEP)
     layer1(HALF)
     ahalo_s[...] = a32[LEN:].astype(BF16)
@@ -253,8 +284,10 @@
     stack("lo", e32, estack, STEP)
     layer1(0)
 
+    pending.append(h_a.wait_send)
     in_copies[6].wait()
     in_copies[7].wait()
+    del pending[:2]
     zero8 = jnp.zeros((8, CH), F32)
 
     def layer2(base, sums):
@@ -288,6 +321,7 @@
     h_g2.start()
     out_bo = pltpu.make_async_copy(bov, block_out, out_sem.at[0])
     out_bo.start()
+    pending += [h_g2.wait_send, out_bo.wait]
 
     owns, xss, xrs, us = (own_a, own_b, own_c), (xs_a, xs_b, xs_c), (xr_a, xr_b, xr_c), (u_a, u_b, u_c)
 
@@ -295,10 +329,13 @@
         return rcopy(xss[g], xrs[g], core_sem.at[2 * g], core_sem.at[2 * g + 1], partner)
 
     def parts_of(g):
-        return (3 * g, 3 * g + 1, 3 * g + 2) if g < 2 else (6,)
+        return (3 * g, 3 * g + 1, 3 * g + 2) if g < 2 else (6, 7)
+
+    def first_row(p):
+        return (p - 3 * min(p // 3, 2)) * (256 if p < 6 else 128)
 
     def order(p):
-        k = p % 3
+        k = (p + (p >= 6)) % 3
         return AXES[k], AXES[(k + 1) % 3], AXES[(k + 2) % 3]
 
     def sems(p, stage):
@@ -306,97 +343,119 @@
 
     def home(p):
         g = min(p // 3, 2)
-        return pl.multiple_of(BASES[g] + s * SPANS[g] + (p - 3 * g) * 256, 256)
-
-    def wait3(p, stage, ref):
+        return pl.multiple_of(BASES[g] + s * SPANS[g] + first_row(p), 128)
+
+    def chunk_rows(p):
+        return 64 if p < 6 else 32
+
+    def cut1(p, n):
+        c = chunk_rows(p)
+        return pl.ds(pl.multiple_of(first_row(p) + n * c, c), c)
+
+    def cut2(ref, n):
+        if ref.shape[0] == 64:
+            return ref.at[pl.ds(pl.multiple_of(n * 16, 16), 16)]
+        return ref.at[:, pl.ds(pl.multiple_of(n * 128, 128), 128)]
+
+    def bufs(p):
+        i = p if p < 6 else p - 6
+        return tuple(r.at[i] for r in ((s1_r, s2_s, s2_r, s3_q) if p < 6 else (c1_r, c2_s, c2_r, c3_q)))
+
+    def chunk_home(p, n):
+        c = chunk_rows(p)
+        return zbuf.at[pl.ds(pl.multiple_of(home(p) + n * c, c), c)]
+
+    def last3(p, stage):
+        if stage == 0:
+            return bufs(p)[0]
+        if stage == 1:
+            return bufs(p)[2]
+        if stage in (2, 3):
+            return bufs(p)[3].at[pl.ds(0, 3)]
+        return zbuf.at[pl.ds(0, 3 * chunk_rows(p))]
+
+    def wait3(p, stage):
         send, recv = sems(p, stage)
-        rcopy(ref, ref, send, recv, partner).wait_recv()
-
-    def wait3_send(p, stage, ref):
-        send, recv = sems(p, stage)
-        rcopy(ref, ref, send, recv, partner).wait_send()
+        rcopy(last3(p, stage), last3(p, stage), send, recv, partner).wait_recv()
+        pending.append(rcopy(last3(p, stage), last3(p, stage), send, recv, partner).wait_send)
 
     def ar_stage0(g):
         core_copy(g).wait_recv()
-        us[g][...] = (owns[g][...] + xrs[g][...].astype(F32)).astype(BF16)
+        pending.append(core_copy(g).wait_send)
+        mine = owns[g][...] if g < 2 else own_c[pl.ds(pl.multiple_of(s * 256, 256), 256)]
+        us[g][...] = (mine + xrs[g][...].astype(F32)).astype(BF16)
         for p in parts_of(g):
-            a = order(p)[0]
             send, recv = sems(p, 0)
             for j in (1, 2, 3):
-                n, to = peer(a, j)
-                off = pl.multiple_of((p - 3 * g) * 256 + n * 64, 64)
-                rcopy(us[g].at[pl.ds(off, 64)], s1_r.at[p, j - 1], send, recv, to).start()
+                n, to = peer(order(p)[0], j)
+                rcopy(us[g].at[cut1(p, n)], bufs(p)[0].at[j - 1], send, recv, to).start()
 
     def ar_stage1(g):
         for p in parts_of(g):
             a, b, _ = order(p)
-            wait3(p, 0, s1_r.at[p])
-            off = pl.multiple_of((p - 3 * g) * 256 + coord[a] * 64, 64)
-            v = us[g][pl.ds(off, 64)].astype(F32)
+            s1, s2s, s2r, _ = bufs(p)
+            wait3(p, 0)
+            v = us[g][cut1(p, coord[a])].astype(F32)
             for j in range(3):
-                v = v + s1_r[p, j].astype(F32)
-            s2_s[p] = v.astype(BF16)
+                v = v + s1[j].astype(F32)
+            s2s[...] = v.astype(BF16)
             send, recv = sems(p, 1)
             for j in (1, 2, 3):
                 n, to = peer(b, j)
-                rcopy(
-                    s2_s.at[p, pl.ds(pl.multiple_of(n * 16, 16), 16)], s2_r.at[p, j - 1], send, recv, to
-                ).start()
+                rcopy(cut2(s2s, n), s2r.at[j - 1], send, recv, to).start()
 
     def ar_stage2(g):
         for p in parts_of(g):
             _, b, c = order(p)
-            wait3(p, 1, s2_r.at[p])
-            v = s2_s[p, pl.ds(pl.multiple_of(coord[b] * 16, 16), 16)].astype(F32)
+            _, s2s, s2r, q = bufs(p)
+            wait3(p, 1)
+            v = cut2(s2s, coord[b])[...].astype(F32)
             for j in range(3):
-                v = v + s2_r[p, j].astype(F32)
-            s3_q[p, coord[c]] = v.astype(BF16)
+                v = v + s2r[j].astype(F32)
+            q[coord[c]] = v.astype(BF16)
             send, recv = sems(p, 2)
             for j in (1, 2, 3):
                 _, to = peer(c, j)
-                rcopy(s3_q.at[p, coord[c]], s3_q.at[p, coord[c]], send, recv, to).start()
+                rcopy(q.at[coord[c]], q.at[coord[c]], send, recv, to).start()
 
     def ar_stage3(g):
         for p in parts_of(g):
-            a, b, c = order(p)
-            wait3(p, 2, s3_q.at[p, pl.ds(0, 3)])
-            q = s3_q[p].astype(F32)
-            at = pl.ds(pl.multiple_of(home(p) + coord[a] * 64 + coord[b] * 16, 16), 16)
-            zbuf[at] = (((q[0] + q[1]) + q[2]) + q[3]).astype(BF16)
+            a, b, _ = order(p)
+            wait3(p, 2)
+            q = bufs(p)[3][...].astype(F32)
+            to_ref = cut2(chunk_home(p, coord[a]), coord[b])
+            to_ref[...] = (((q[0] + q[1]) + q[2]) + q[3]).astype(BF16)
             send, recv = sems(p, 3)
             for j in (1, 2, 3):
                 _, to = peer(b, j)
-                rcopy(zbuf.at[at], zbuf.at[at], send, recv, to).start()
+                rcopy(to_ref, to_ref, send, recv, to).start()
 
     def ar_stage4(g):
         for p in parts_of(g):
-            a, b, c = order(p)
-            wait3(p, 3, zbuf.at[pl.ds(0, 48)])
-            at = pl.ds(pl.multiple_of(home(p) + coord[a] * 64, 64), 64)
+            a = order(p)[0]
+            wait3(p, 3)
+            ref = chunk_home(p, coord[a])
             send, recv = sems(p, 4)
             for j in (1, 2, 3):
                 _, to = peer(a, j)
-                rcopy(zbuf.at[at], zbuf.at[at], send, recv, to).start()
+                rcopy(ref, ref, send, recv, to).start()
+
+    def last_copy(p):
+        ref = zbuf.at[pl.ds(home(p), 4 * chunk_rows(p))]
+        return rcopy(ref, ref, fin_sem.at[2 * p], fin_sem.at[2 * p + 1], partner)
 
     def ar_stage5(g):
         for p in parts_of(g):
-            wait3(p, 4, zbuf.at[pl.ds(0, 192)])
-            at = pl.ds(home(p), 256)
-            rcopy(zbuf.at[at], zbuf.at[at], fin_sem.at[2 * p], fin_sem.at[2 * p + 1], partner).start()
+            wait3(p, 4)
+            last_copy(p).start()
 
     def ar_finish(g):
         for p in parts_of(g):
-            at = pl.ds(home(p), 256)
-            rcopy(zbuf.at[at], zbuf.at[at], fin_sem.at[2 * p], fin_sem.at[2 * p + 1], partner).wait()
-
-    def ar_drain(g):
-        core_copy(g).wait_send()
-        for p in parts_of(g):
-            wait3_send(p, 0, s1_r.at[p])
-            wait3_send(p, 1, s2_r.at[p])
-            wait3_send(p, 2, s3_q.at[p, pl.ds(0, 3)])
-            wait3_send(p, 3, zbuf.at[pl.ds(0, 48)])
-            wait3_send(p, 4, zbuf.at[pl.ds(0, 192)])
+            last_copy(p).wait()
+        at = pl.ds(BASES[g], 2 * SPANS[g])
+        c = pltpu.make_async_copy(zbuf.at[at], grads.at[at], out_sem.at[5 + g])
+        c.start()
+        pending.append(c.wait)
 
     def weight_sum(g, taps, gb):
         theirs = pl.ds(pl.multiple_of(other * 768, 256), 768)
@@ -430,15 +489,16 @@
     ghalo1_s[...] = g1f[0:16].astype(BF16)
     h_g1 = halo(3, ghalo1_s, ghalo1_r)
     h_g1.start()
+    pending.append(h_g1.wait_send)
     ar_stage0(0)
     h_g2.wait_recv()
     g2f[LEN:] = jnp.where(first_core, ghalo2_r[...].astype(F32), 0.0)
     sums1 = back1(HALF, sums1)
-    ar_stage1(0)
     weight_sum(1, estack, g1f[0:LEN].astype(BF16))
     h_g1.wait_recv()
     g1f[LEN:] = jnp.where(first_core, ghalo1_r[...].astype(F32)[0:8], 0.0)
-    ar_stage2(0)
+    ar_stage1(0)
+    ar_stage0(1)
 
     for base in (0, HALF):
         ge[base : base + HALF] = (
@@ -448,55 +508,51 @@
                 for k in range(3)
             )
         ).astype(BF16)
+
+    own_c[...] = dot(xm[...], ge[...], TN)
+    own_c[480:488] = jnp.concatenate(
+        [jnp.sum(v, axis=0, keepdims=True) for v in (*sums1, *sums2)] + [jnp.zeros((2, CH), F32)], axis=0
+    )
+    xs_c[...] = own_c[pl.ds(pl.multiple_of(other * 256, 256), 256)].astype(BF16)
+    core_copy(2).start()
+    ar_stage2(0)
+
     rg = dot(ge[...], pext[...], NT)
     first = jnp.where(eb == 0.0, rg[:, 0:128], jnp.where(eb == 1.0, rg[:, 256:384], rg[:, 384:512]))
     rgb = jnp.concatenate([first, rg[:, 128:256]], axis=1).astype(BF16)
-    slots = dot(place[...], rgb, TN)
+    slots = dot(place[...], rgb)
     gmsg[...] = jnp.concatenate(
         [slots[:, 0:128].reshape(NDEV, 8, 128), slots[:, 128:256].reshape(NDEV, 8, 128)], axis=1
     ).astype(BF16)
+    ar_stage0(2)
 
     def send_grad(k, c):
         to = lax.rem(me + k, NDEV)
         rcopy(gmsg.at[to], gotg.at[me], gr_sem.at[0], gr_sem.at[1], dev(to)).start()
         return c
 
-    ar_stage0(1)
-    lax.fori_loop(1, NDEV, send_grad, 0)
+    lax.fori_loop(1, 43, send_grad, 0)
     own = pltpu.make_async_copy(gmsg.at[me], gotg.at[me], loc_sem.at[0])
     own.start()
-
-    pg = dot(xm[...], ge[...], TN)
-    owns_full = hid
-    vec = jnp.concatenate(
-        [jnp.sum(v, axis=0, keepdims=True) for v in (*sums1, *sums2)] + [jnp.zeros((2, CH), F32)], axis=0
-    )
-    own_c[...] = pg
-    own_c[480:488] = vec
-    xs_c[...] = own_c[pl.ds(pl.multiple_of(other * 256, 256), 256)].astype(BF16)
-    core_copy(2).start()
+    ar_stage1(1)
     ar_stage3(0)
-    ar_stage1(1)
-
-    core_copy(2).wait_recv()
-    u_c[...] = (own_c[pl.ds(pl.multiple_of(s * 256, 256), 256)] + xr_c[...].astype(F32)).astype(BF16)
-    a6 = order(6)[0]
-    for j in (1, 2, 3):
-        n, to = peer(a6, j)
-        send, recv = sems(6, 0)
-        rcopy(u_c.at[pl.ds(pl.multiple_of(n * 64, 64), 64)], s1_r.at[6, j - 1], send, recv, to).start()
+    lax.fori_loop(43, 86, send_grad, 0)
+    ar_stage1(2)
+    ar_stage2(1)
+    lax.fori_loop(86, NDEV, send_grad, 0)
     ar_stage4(0)
-    ar_stage2(1)
-    ar_stage1(2)
+    ar_stage2(2)
+    ar_stage3(1)
+    ar_stage3(2)
+    ar_stage4(1)
     ar_stage5(0)
-    ar_stage3(1)
-    ar_stage2(2)
-    ar_stage4(1)
-    ar_stage3(2)
+    ar_stage4(2)
 
     own.wait()
     wg = rcopy(gmsg.at[pl.ds(0, 127)], gotg.at[pl.ds(0, 127)], gr_sem.at[0], gr_sem.at[1], partner)
     wg.wait_recv()
+    pending.append(wg.wait_send)
+    ar_finish(0)
     band = code_sc[...] >> 11
     lane_s = lax.broadcasted_iota(I32, (SLOTS, 128), 1)
     both = gotg[...].astype(F32)
@@ -512,29 +568,16 @@
         (tout.at[0:256], t_wide), (tout.at[256:384], t_mid),
         (tout.at[384:448], t_narrow), (tout.at[448:480], t_thin),
     ]
-    out_copies = [pltpu.make_async_copy(a, b, out_sem.at[1 + i]) for i, (a, b) in enumerate(outs)]
-    for c in out_copies:
+    for i, (a, b) in enumerate(outs):
+        c = pltpu.make_async_copy(a, b, out_sem.at[1 + i])
         c.start()
+        pending.append(c.wait)
 
     ar_stage5(1)
-    ar_stage4(2)
     ar_stage5(2)
-    for g in range(3):
-        ar_finish(g)
-    out_z = pltpu.make_async_copy(zbuf, grads, out_sem.at[5])
-    out_z.start()
-    for g in range(3):
-        ar_drain(g)
-    rcopy(relay.at[pl.ds(0, 7)], relay.at[pl.ds(0, 7)], rq_sem.at[0], rq_sem.at[1], partner).wait_send()
-    w2nd.wait_send()
-    wa.wait_send()
-    wg.wait_send()
-    for h in (h_e, h_a, h_g2, h_g1):
-        h.wait_send()
-    out_bo.wait()
-    for c in out_copies:
-        c.wait()
-    out_z.wait()
+    ar_finish(1)
+    ar_finish(2)
+    finish()
 
 
 def scratch():
@@ -542,8 +585,8 @@
     dma = pltpu.SemaphoreType.DMA
     return [
         v((512, ROWS), BF16), v((512, CH), BF16), v((1536, CH), BF16), v((1536, CH), BF16), v((LEN, CH), BF16),
-        v((8, 16, 1, 128), I32), v((16, 8, 1, 128), I32), v((SLOTS, 128), I32), v((SLOTS, ROWS), BF16),
-        v((LEN, SLOTS), BF16), v((NDEV, 16, 128), BF16), v((NDEV, 16, 128), BF16),
+        v((8, 1, 128), I32), v((8, 1, 128), I32), v((16, 8, 128), I32), v((16, 8, 128), I32), v((SLOTS, 128), I32), v((SLOTS, ROWS), BF16),
+        v((SLOTS, LEN), BF16), v((SLOTS, 384), BF16), v((NDEV, 16, 128), BF16), v((NDEV, 16, 128), BF16),
         v((LEN, 128), F32), v((LEN, 512), BF16), v((8 + LEN, CH), F32), v((16, CH), BF16), v((16, CH), BF16),
         v((LEN, 1536), BF16), v((HALF, CH), F32), v((LEN, CH), F32), v((LEN, CH), F32), v((LEN, 128), F32),
         v((16 + LEN, CH), F32), v((16, CH), BF16), v((16, CH), BF16), v((LEN, 1536), BF16),
@@ -554,9 +597,10 @@
         v((768, CH), BF16), v((768, CH), BF16), v((256, CH), BF16),
         v((768, CH), BF16), v((768, CH), BF16), v((256, CH), BF16),
         v((768, CH), BF16), v((768, CH), BF16), v((256, CH), BF16),
-        v((7, 3, 64, CH), BF16), v((7, 64, CH), BF16), v((7, 3, 16, CH), BF16), v((7, 4, 16, CH), BF16),
+        v((6, 3, 64, CH), BF16), v((6, 64, CH), BF16), v((6, 3, 16, CH), BF16), v((6, 4, 16, CH), BF16),
+        v((2, 3, 32, CH), BF16), v((2, 32, CH), BF16), v((2, 3, 32, 128), BF16), v((2, 4, 32, 128), BF16),
         v((3584, CH), BF16),
-        dma((8,)), dma((4,)), dma((2,)), dma((8,)), dma((2,)), dma((6,)), dma((70,)), dma((14,)), dma((6,)), dma((1,)),
+        dma((8,)), dma((4,)), dma((2,)), dma((8,)), dma((2,)), dma((6,)), dma((80,)), dma((16,)), dma((8,)), dma((1,)),
     ]
 
 
@@ -565,11 +609,7 @@
     gain_first, offset_first, second_conv_weight, second_conv_bias, gain_second, offset_second,
     slot_event, slot_counts, slot_band, slot_row, out_grad,
 ):
-    live = jnp.arange(CAP, dtype=I32)[None, :] < slot_counts[0, 0][:, None]
-    code = slot_row[0, 0] + ROWS * slot_band[0, 0]
-    codes = jnp.pad(code, ((0, 0), (0, 128 - CAP))).reshape(16, 8, 1, 128)
-    target = jnp.where(live, slot_event[0, 0], LEN).reshape(1, SLOTS)
-    sband = slot_band[0, 0].reshape(1, SLOTS)
+    across = [v[0, 0].T for v in (slot_row, slot_band, slot_event)]
     vecs = [
         v.reshape(1, CH)
         for v in (first_conv_bias, gain_first, offset_first, second_conv_bias, gain_second, offset_second)
@@ -582,7 +622,7 @@
             sds((LEN, CH), BF16), sds((256, ROWS), BF16), sds((128, ROWS), BF16), sds((64, ROWS), BF16),
             sds((32, ROWS), BF16), sds((3584, CH), BF16),
         ],
-        in_specs=[hbm] * 8 + [vmem] * 9,
+        in_specs=[hbm] * 8 + [vmem] * 10,
         out_specs=[hbm] * 6,
         scratch_shapes=scratch(),
         compiler_params=pltpu.CompilerParams(
@@ -591,22 +631,70 @@
         cost_estimate=pl.CostEstimate(flops=12 * 10**9, bytes_accessed=14 * 2**20, transcendentals=2**19),
     )(
         table_wide, table_mid, table_narrow, table_thin, band_proj, first_conv_weight, second_conv_weight,
-        out_grad[0], codes, target, sband, *vecs,
+        out_grad[0], *across, slot_counts[0], *vecs,
     )
+    copied = [block_out, tw, tm, tn, tt]
+    outs = pl.pallas_call(
+        finish_kernel,
+        out_shape=[sds(v.shape, v.dtype) for v in copied]
+        + [sds((480, CH), F32), sds((1536, CH), F32), sds((1536, CH), F32), sds((6, CH), F32)],
+        in_specs=[hbm] * 6,
+        out_specs=[hbm] * 9,
+        scratch_shapes=[pltpu.VMEM(v.shape, v.dtype) for v in copied]
+        + [
+            pltpu.VMEM((3584, CH), BF16), pltpu.VMEM((3584, CH), F32), pltpu.VMEM((6, CH), F32),
+            pltpu.SemaphoreType.DMA((5,)), pltpu.SemaphoreType.DMA((7,)), pltpu.SemaphoreType.DMA((8,)), pltpu.SemaphoreType.DMA((5,)),
+        ],
+        compiler_params=pltpu.CompilerParams(vmem_limit_bytes=60 << 20),
+    )(*copied, grads)
+    return (outs[0][None], *outs[1:])
+
+
+def finish_kernel(*refs):
+    copied, z, outs = refs[:5], refs[5], refs[6:15]
+    held = refs[15:20]
+    zb, zf, vec, cs, zs, os_, ds = refs[20:]
+    loads = [
+        pltpu.make_async_copy(z.at[i * 512 : (i + 1) * 512], zb.at[i * 512 : (i + 1) * 512], zs.at[i])
+        for i in range(7)
+    ]
+    arrivals = [pltpu.make_async_copy(a, b, cs.at[i]) for i, (a, b) in enumerate(zip(copied, held))]
+    for c in loads[:4] + arrivals + loads[4:]:
+        c.start()
+    moves = []
     scale = 1.0 / float(NDEV * LEN) ** 0.5
-    wide_grads = grads.astype(F32) * scale
-    return (
-        block_out[None], tw, tm, tn, tt, wide_grads[3072:3552], wide_grads[1536:3072], wide_grads[0:1536],
-        wide_grads[3552:3558],
-    )
+    proj, c1, c2, vout = outs[5:]
+    for i in range(7):
+        loads[i].wait()
+        at = slice(i * 512, (i + 1) * 512)
+        zf[at] = zb[at].astype(F32) * scale
+        if i < 6:
+            to = (c2 if i < 3 else c1).at[(i % 3) * 512 : (i % 3 + 1) * 512]
+            c = pltpu.make_async_copy(zf.at[at], to, os_.at[i])
+        else:
+            c = pltpu.make_async_copy(zf.at[3072:3552], proj, os_.at[i])
+        c.start()
+        moves.append(c)
+        if 1 < i < 7:
+            arrivals[i - 2].wait()
+            c = pltpu.make_async_copy(held[i - 2], outs[i - 2], ds.at[i - 2])
+            c.start()
+            moves.append(c)
+    vec[...] = zf[3552:3558]
+    c = pltpu.make_async_copy(vec, vout, os_.at[7])
+    c.start()
+    for c in moves + [c]:
+        c.wait()
+
+
+ROW_SPLIT = P(None, ("table", "seq", "dp"))
+HIST = ("table", "dp")
+IN_SPECS = (ROW_SPLIT,) * 4 + (P(),) * 9 + (
+    P(HIST, "seq", None, None), P(HIST, "seq", None), P(HIST, "seq", None, None), P(HIST, "seq", None, None),
+    P(HIST, "seq", None),
+)
+OUT_SPECS = (P(HIST, "seq", None),) + (ROW_SPLIT,) * 4 + (P(),) * 4
 
 
 def solution(mesh):
-    rows = P(None, ("table", "seq", "dp"))
-    hist = ("table", "dp")
-    in_specs = (rows,) * 4 + (P(),) * 9 + (
-        P(hist, "seq", None, None), P(hist, "seq", None), P(hist, "seq", None, None), P(hist, "seq", None, None),
-        P(hist, "seq", None),
-    )
-    out_specs = (P(hist, "seq", None),) + (rows,) * 4 + (P(),) * 4
-    return jax.shard_map(shards, mesh=mesh, in_specs=in_specs, out_specs=out_specs, check_vma=False)
+    return jax.shard_map(shards, mesh=mesh, in_specs=IN_SPECS, out_specs=OUT_SPECS, check_vma=False)

time: 112 us -> 86.6 us (0.77)
  local copies, waits for them, and re-layouts: 12.2 us -> 0 us
  Pallas kernels: 93.6 us -> 85.7 us
  other arithmetic: 5.12 us -> 0 us
    pallas_call x1, Pallas kernels: 93.6 us -> 79.9 us  [shards(): pl.pallas_call(kernel, out_shape=[sds((LEN, CH), BF16), sds((256, ROWS),...]
    pallas_call x0 -> x1, Pallas kernels: none -> 5.75 us  [shards(): pl.pallas_call(finish_kernel, out_shape=[sds(v.shape, v.dtype) for v in c...]
    unnamed x18 -> x0, local copies, waits for them, and re-layouts: 5.61 us -> none
    slice x3 -> x0, local copies, waits for them, and re-layouts: 5.03 us -> none  [the longest x1 3.41 us: shards(): wide_grads[0:1536]]
    mul x1 -> x0, other arithmetic: 3.08 us -> none  [shards(): wide_grads = grads.astype(F32) * scale]
where the time goes in v1:
time: 86.6 us; the launch traced here: 86.5 us
  Pallas kernels  85.7 us (99%)
    pallas_call x1, Pallas kernels, shards(): pl.pallas_call(kernel, out_shape=[sds((LEN, CH), BF16), sds((256, ROWS),...  79.9 us
    pallas_call x1, Pallas kernels, shards(): pl.pallas_call(finish_kernel, out_shape=[sds(v.shape, v.dtype) for v in c...  5.75 us

profile of v1, /device:TPU:1, one launch (start us, length us, event | category | flops | bytes accessed | tf_op | source)
XLA Modules:
  0.0 86.5 jit_solution(18439998016421649773)
XLA Ops:
  0.6 79.9 %shard_map.241 = (bf16[512,512]{1,0:T(8,128)(2,1)}, bf16[256,2048]{1,0:T(8,128)(2,1)}, bf16[128,2048]{1,0:T(8,128)(2,1)}, bf16[64,2048]{1,0:T(8,128)(2,1)}, bf16...) custom-call(bf16[256,2048]{1,0:T(8,128)(2,1)} %wide.1, bf16[128,2048]{1,0:T(8,128)(2,1)} %mid.1, bf16[64,2048]{1,0:T(8,128)(2,1)} %narrow.1, ...), custom_call_target="tpu_custom_call" | custom-call | flops 12000000000 | bytes 14680064 | tf_op jit(solution)/shard_map/pallas_call | solution.py:619
  80.6 5.8 %shard_map.242 = (bf16[512,512]{1,0:T(8,128)(2,1)}, bf16[256,2048]{1,0:T(8,128)(2,1)}, bf16[128,2048]{1,0:T(8,128)(2,1)}, bf16[64,2048]{1,0:T(8,128)(2,1)}, bf16...) custom-call(bf16[512,512]{1,0:T(8,128)(2,1)} %get-tuple-element.24.r, ...), custom_call_target="tpu_custom_call" | custom-call | tf_op jit(solution)/shard_map/pallas_call | solution.py:637

commit v2 on v1

--- a/solution.py
+++ b/solution.py
@@ -65,11 +65,11 @@
     wide, mid, narrow, thin, proj, w1, w2, og,
     srow, sbandr, sevent, scount, b1, g1, o1, b2, g2, o2,
     block_out, t_wide, t_mid, t_narrow, t_thin, grads,
-    tcat, pext, w1v, w2v, ogv, codes, relay, passed, fetched, code_sc, onehot, place, xin, msg, answers,
+    tcat, pext, w1v, w2v, w1t, w2t, ogv, codes, relay, passed, fetched, code_sc, onehot, place, xin, msg, answers,
     eband, xm, e32, ehalo_s, ehalo_r, estack, hid, norm1, slope1, rstd1, a32, ahalo_s, ahalo_r, astack,
     bov, g2f, ghalo2_s, ghalo2_r, g1f, ghalo1_s, ghalo1_r, ge, gmsg, gotg, mt, tout,
     own_a, own_b, own_c, xs_a, xs_b, xs_c, xr_a, xr_b, xr_c, u_a, u_b, u_c,
-    s1_r, s2_s, s2_r, s3_q, c1_r, c2_s, c2_r, c3_q, zbuf,
+    s1_r, s2_s, s2_r, s3_q, c1_r, c2_s, c2_r, c3_q, plane_r, zbuf,
     in_sem, rq_sem, ans_sem, halo_sem, gr_sem, core_sem, ar_sem, fin_sem, out_sem, loc_sem,
 ):
     t, s, d = lax.axis_index("table"), lax.axis_index("seq"), lax.axis_index("dp")
@@ -86,6 +86,13 @@
             return n, (t, s, n)
         return n, (n * 4 + coord["x"], s, d)
 
+    def plane(b, c):
+        for jb in range(4):
+            for jc in range(4):
+                if jb or jc:
+                    n = {a: lax.rem(coord[a] + jb * (a == b) + jc * (a == c), 4) for a in AXES}
+                    yield jb * 4 + jc - 1, n[b], n[c], (n["z"] * 4 + n["x"], s, n["y"])
+
     def dev(o):
         return (o // 8, lax.rem(o // 4, 2), lax.rem(o, 4))
 
@@ -174,7 +181,7 @@
 
     lane128 = lax.broadcasted_iota(I32, (HALF, 128), 1)
 
-    def lookup(i, carry):
+    def lookup(i):
         cb = lax.rem(me // 32 + i, 4)
         rows = pl.ds(pl.multiple_of(cb * HALF, HALF), HALF)
         code = code_sc[rows]
@@ -190,18 +197,17 @@
         )
         msg[pl.ds(cb * 32, 32)] = both.astype(BF16)
 
-        def send(k, c):
+    def answer(i):
+        cb = lax.rem(me // 32 + i, 4)
+        for k in range(0 if i else 1, 32):
             to = cb * 32 + lax.rem(me + k, 32)
-
-            @pl.when(to != me)
-            def _():
-                rcopy(msg.at[to], answers.at[me], ans_sem.at[0], ans_sem.at[1], dev(to)).start()
-
-            return c
-
-        return lax.fori_loop(0, 32, send, carry)
-
-    lax.fori_loop(0, 4, lookup, 0)
+            rcopy(msg.at[to], answers.at[me], ans_sem.at[0], ans_sem.at[1], dev(to)).start()
+
+    lookup(0)
+    for i in range(4):
+        answer(i)
+        if i < 3:
+            lookup(i + 1)
 
     live = lax.broadcasted_iota(I32, (CAP, NDEV), 0) < scount[...]
     target = spread(turned(jnp.where(live, sevent[...], LEN).astype(F32)).reshape(NDEV, 1, 128)).astype(I32)
@@ -209,9 +215,14 @@
     for b in range(4):
         place[:, b * 128 : (b + 1) * 128] = (target == lane_p + b * 128).astype(F32).astype(BF16)
     xin[:, 256:384] = spread(turned(sbandr[...].astype(F32)).reshape(NDEV, 1, 128)).astype(BF16)
-    own = pltpu.make_async_copy(msg.at[me], answers.at[me], loc_sem.at[0])
-    own.start()
-    own.wait()
+    answers[me] = msg[me]
+    for c in in_copies[5:7]:
+        c.wait()
+    del pending[1:3]
+    for k in range(3):
+        at = slice(k * CH, (k + 1) * CH)
+        w1t[at] = w1v[at].T
+        w2t[at] = w2v[at].T
     wa = rcopy(msg.at[pl.ds(0, 127)], answers.at[pl.ds(0, 127)], ans_sem.at[0], ans_sem.at[1], partner)
     wa.wait_recv()
     pending.append(wa.wait_send)
@@ -272,8 +283,6 @@
         lax.fori_loop(0, HALF // BLK, block, 0)
 
     pending.append(h_e.wait_send)
-    in_copies[5].wait()
-    del pending[0]
     stack("hi", e32, estack, STEP)
     layer1(HALF)
     ahalo_s[...] = a32[LEN:].astype(BF16)
@@ -285,9 +294,8 @@
     layer1(0)
 
     pending.append(h_a.wait_send)
-    in_copies[6].wait()
     in_copies[7].wait()
-    del pending[:2]
+    del pending[0]
     zero8 = jnp.zeros((8, CH), F32)
 
     def layer2(base, sums):
@@ -379,6 +387,28 @@
         rcopy(last3(p, stage), last3(p, stage), send, recv, partner).wait_recv()
         pending.append(rcopy(last3(p, stage), last3(p, stage), send, recv, partner).wait_send)
 
+    def tile(ref, i, j):
+        return ref.at[pl.ds(pl.multiple_of(i * 16, 16), 16), pl.ds(pl.multiple_of(j * 128, 128), 128)]
+
+    def wait15(p, stage):
+        send, recv = sems(p, stage)
+        ref = plane_r.at[p - 3]
+        rcopy(ref, ref, send, recv, partner).wait_recv()
+        pending.append(rcopy(ref, ref, send, recv, partner).wait_send)
+
+    def plane_sum():
+        for p in parts_of(1):
+            a, b, c = order(p)
+            wait15(p, 1)
+            v = tile(s2_s.at[p], coord[b], coord[c])[...].astype(F32)
+            for i in range(15):
+                v = v + plane_r[p - 3, i].astype(F32)
+            ref = tile(chunk_home(p, coord[a]), coord[b], coord[c])
+            ref[...] = v.astype(BF16)
+            send, recv = sems(p, 3)
+            for _, _, _, to in plane(b, c):
+                rcopy(ref, ref, send, recv, to).start()
+
     def ar_stage0(g):
         core_copy(g).wait_recv()
         pending.append(core_copy(g).wait_send)
@@ -400,6 +430,10 @@
                 v = v + s1[j].astype(F32)
             s2s[...] = v.astype(BF16)
             send, recv = sems(p, 1)
+            if g == 1:
+                for i, nb, nc, to in plane(b, order(p)[2]):
+                    rcopy(tile(s2s, nb, nc), plane_r.at[p - 3, i], send, recv, to).start()
+                continue
             for j in (1, 2, 3):
                 n, to = peer(b, j)
                 rcopy(cut2(s2s, n), s2r.at[j - 1], send, recv, to).start()
@@ -433,7 +467,7 @@
     def ar_stage4(g):
         for p in parts_of(g):
             a = order(p)[0]
-            wait3(p, 3)
+            (wait15 if g == 1 else wait3)(p, 3)
             ref = chunk_home(p, coord[a])
             send, recv = sems(p, 4)
             for j in (1, 2, 3):
@@ -448,14 +482,21 @@
         for p in parts_of(g):
             wait3(p, 4)
             last_copy(p).start()
+            write_out(p, s)
+
+    def write_out(p, core):
+        g = min(p // 3, 2)
+        at = pl.ds(pl.multiple_of(BASES[g] + core * SPANS[g] + first_row(p), 128), 4 * chunk_rows(p))
+        i = 5 + 2 * p
+        sem = out_sem.at[i] if core is s else out_sem.at[i + 1]
+        c = pltpu.make_async_copy(zbuf.at[at], grads.at[at], sem)
+        c.start()
+        pending.append(c.wait)
 
     def ar_finish(g):
         for p in parts_of(g):
             last_copy(p).wait()
-        at = pl.ds(BASES[g], 2 * SPANS[g])
-        c = pltpu.make_async_copy(zbuf.at[at], grads.at[at], out_sem.at[5 + g])
-        c.start()
-        pending.append(c.wait)
+            write_out(p, other)
 
     def weight_sum(g, taps, gb):
         theirs = pl.ds(pl.multiple_of(other * 768, 256), 768)
@@ -468,7 +509,7 @@
 
     def back1(base, sums):
         hid[...] = sum(
-            dot(g2f[base + k * 8 : base + k * 8 + HALF].astype(BF16), w2v[k * CH : (k + 1) * CH], NT)
+            dot(g2f[base + k * 8 : base + k * 8 + HALF].astype(BF16), w2t[k * CH : (k + 1) * CH])
             for k in range(3)
         )
 
@@ -497,17 +538,20 @@
     weight_sum(1, estack, g1f[0:LEN].astype(BF16))
     h_g1.wait_recv()
     g1f[LEN:] = jnp.where(first_core, ghalo1_r[...].astype(F32)[0:8], 0.0)
-    ar_stage1(0)
-    ar_stage0(1)
-
-    for base in (0, HALF):
+
+    def embed_grad(base):
         ge[base : base + HALF] = (
             ogv[base : base + HALF].astype(F32)
             + sum(
-                dot(g1f[base + k * 4 : base + k * 4 + HALF].astype(BF16), w1v[k * CH : (k + 1) * CH], NT)
+                dot(g1f[base + k * 4 : base + k * 4 + HALF].astype(BF16), w1t[k * CH : (k + 1) * CH])
                 for k in range(3)
             )
         ).astype(BF16)
+
+    embed_grad(0)
+    ar_stage0(1)
+    embed_grad(HALF)
+    ar_stage1(0)
 
     own_c[...] = dot(xm[...], ge[...], TN)
     own_c[480:488] = jnp.concatenate(
@@ -515,7 +559,6 @@
     )
     xs_c[...] = own_c[pl.ds(pl.multiple_of(other * 256, 256), 256)].astype(BF16)
     core_copy(2).start()
-    ar_stage2(0)
 
     rg = dot(ge[...], pext[...], NT)
     first = jnp.where(eb == 0.0, rg[:, 0:128], jnp.where(eb == 1.0, rg[:, 256:384], rg[:, 384:512]))
@@ -524,57 +567,54 @@
     gmsg[...] = jnp.concatenate(
         [slots[:, 0:128].reshape(NDEV, 8, 128), slots[:, 128:256].reshape(NDEV, 8, 128)], axis=1
     ).astype(BF16)
-    ar_stage0(2)
-
     def send_grad(k, c):
         to = lax.rem(me + k, NDEV)
         rcopy(gmsg.at[to], gotg.at[me], gr_sem.at[0], gr_sem.at[1], dev(to)).start()
         return c
 
-    lax.fori_loop(1, 43, send_grad, 0)
-    own = pltpu.make_async_copy(gmsg.at[me], gotg.at[me], loc_sem.at[0])
-    own.start()
+    gotg[me] = gmsg[me]
+
+    def scatter():
+        wg = rcopy(gmsg.at[pl.ds(0, 127)], gotg.at[pl.ds(0, 127)], gr_sem.at[0], gr_sem.at[1], partner)
+        wg.wait_recv()
+        pending.append(wg.wait_send)
+        band = code_sc[...] >> 11
+        lane_s = lax.broadcasted_iota(I32, (SLOTS, 128), 1)
+        both = gotg[...].astype(F32)
+        h0, h1 = both[:, 0:8].reshape(SLOTS, 128), both[:, 8:16].reshape(SLOTS, 128)
+        tail = ((band == 2) & (lane_s < 64)) | ((band == 3) & (lane_s >= 64) & (lane_s < 96))
+        mt[0:128] = jnp.where(band == 0, h0, 0.0).T.astype(BF16)
+        mt[128:256] = jnp.where(band == 0, h1, 0.0).T.astype(BF16)
+        mt[256:384] = jnp.where(band == 1, h0, 0.0).T.astype(BF16)
+        mt[384:512] = jnp.where(tail, h0, 0.0).T.astype(BF16)
+        for b in range(4):
+            tout[:, b * 512 : (b + 1) * 512] = dot(mt[...], onehot[:, b * 512 : (b + 1) * 512]).astype(BF16)
+        outs = [
+            (tout.at[0:256], t_wide), (tout.at[256:384], t_mid),
+            (tout.at[384:448], t_narrow), (tout.at[448:480], t_thin),
+        ]
+        for i, (a, b) in enumerate(outs):
+            c = pltpu.make_async_copy(a, b, out_sem.at[1 + i])
+            c.start()
+            pending.append(c.wait)
+
+    lax.fori_loop(1, NDEV, send_grad, 0)
+    ar_stage2(0)
+    ar_stage0(2)
     ar_stage1(1)
     ar_stage3(0)
-    lax.fori_loop(43, 86, send_grad, 0)
     ar_stage1(2)
-    ar_stage2(1)
-    lax.fori_loop(86, NDEV, send_grad, 0)
+    plane_sum()
+    ar_stage2(2)
     ar_stage4(0)
-    ar_stage2(2)
-    ar_stage3(1)
     ar_stage3(2)
     ar_stage4(1)
+    scatter()
+    ar_stage4(2)
     ar_stage5(0)
-    ar_stage4(2)
-
-    own.wait()
-    wg = rcopy(gmsg.at[pl.ds(0, 127)], gotg.at[pl.ds(0, 127)], gr_sem.at[0], gr_sem.at[1], partner)
-    wg.wait_recv()
-    pending.append(wg.wait_send)
-    ar_finish(0)
-    band = code_sc[...] >> 11
-    lane_s = lax.broadcasted_iota(I32, (SLOTS, 128), 1)
-    both = gotg[...].astype(F32)
-    h0, h1 = both[:, 0:8].reshape(SLOTS, 128), both[:, 8:16].reshape(SLOTS, 128)
-    tail = ((band == 2) & (lane_s < 64)) | ((band == 3) & (lane_s >= 64) & (lane_s < 96))
-    mt[0:128] = jnp.where(band == 0, h0, 0.0).T.astype(BF16)
-    mt[128:256] = jnp.where(band == 0, h1, 0.0).T.astype(BF16)
-    mt[256:384] = jnp.where(band == 1, h0, 0.0).T.astype(BF16)
-    mt[384:512] = jnp.where(tail, h0, 0.0).T.astype(BF16)
-    for b in range(4):
-        tout[:, b * 512 : (b + 1) * 512] = dot(mt[...], onehot[:, b * 512 : (b + 1) * 512]).astype(BF16)
-    outs = [
-        (tout.at[0:256], t_wide), (tout.at[256:384], t_mid),
-        (tout.at[384:448], t_narrow), (tout.at[448:480], t_thin),
-    ]
-    for i, (a, b) in enumerate(outs):
-        c = pltpu.make_async_copy(a, b, out_sem.at[1 + i])
-        c.start()
-        pending.append(c.wait)
-
     ar_stage5(1)
     ar_stage5(2)
+    ar_finish(0)
     ar_finish(1)
     ar_finish(2)
     finish()
@@ -584,7 +624,7 @@
     v = pltpu.VMEM
     dma = pltpu.SemaphoreType.DMA
     return [
-        v((512, ROWS), BF16), v((512, CH), BF16), v((1536, CH), BF16), v((1536, CH), BF16), v((LEN, CH), BF16),
+        v((512, ROWS), BF16), v((512, CH), BF16), v((1536, CH), BF16), v((1536, CH), BF16), v((1536, CH), BF16), v((1536, CH), BF16), v((LEN, CH), BF16),
         v((8, 1, 128), I32), v((8, 1, 128), I32), v((16, 8, 128), I32), v((16, 8, 128), I32), v((SLOTS, 128), I32), v((SLOTS, ROWS), BF16),
         v((SLOTS, LEN), BF16), v((SLOTS, 384), BF16), v((NDEV, 16, 128), BF16), v((NDEV, 16, 128), BF16),
         v((LEN, 128), F32), v((LEN, 512), BF16), v((8 + LEN, CH), F32), v((16, CH), BF16), v((16, CH), BF16),
@@ -599,8 +639,8 @@
         v((768, CH), BF16), v((768, CH), BF16), v((256, CH), BF16),
         v((6, 3, 64, CH), BF16), v((6, 64, CH), BF16), v((6, 3, 16, CH), BF16), v((6, 4, 16, CH), BF16),
         v((2, 3, 32, CH), BF16), v((2, 32, CH), BF16), v((2, 3, 32, 128), BF16), v((2, 4, 32, 128), BF16),
-        v((3584, CH), BF16),
-        dma((8,)), dma((4,)), dma((2,)), dma((8,)), dma((2,)), dma((6,)), dma((80,)), dma((16,)), dma((8,)), dma((1,)),
+        v((3, 15, 16, 128), BF16), v((3584, CH), BF16),
+        dma((8,)), dma((4,)), dma((2,)), dma((8,)), dma((2,)), dma((6,)), dma((80,)), dma((16,)), dma((21,)), dma((1,)),
     ]
 
 

time: 86.6 us -> 84.8 us (0.979)
  Pallas kernels: 85.7 us -> 83.8 us
    pallas_call x1, Pallas kernels: 79.9 us -> 78 us  [shards(): pl.pallas_call(kernel, out_shape=[sds((LEN, CH), BF16), sds((256, ROWS),...]
where the time goes in v2:
time: 84.8 us; the launch traced here: 84.6 us
  Pallas kernels  83.8 us (99%)
    pallas_call x1, Pallas kernels, shards(): pl.pallas_call(kernel, out_shape=[sds((LEN, CH), BF16), sds((256, ROWS),...  78 us
    pallas_call x1, Pallas kernels, shards(): pl.pallas_call(finish_kernel, out_shape=[sds(v.shape, v.dtype) for v in c...  5.75 us

profile of v2, /device:TPU:1, one launch (start us, length us, event | category | flops | bytes accessed | tf_op | source)
XLA Modules:
  0.0 84.6 jit_solution(9468116028478226993)
XLA Ops:
  0.6 78.0 %shard_map.241 = (bf16[512,512]{1,0:T(8,128)(2,1)}, bf16[256,2048]{1,0:T(8,128)(2,1)}, bf16[128,2048]{1,0:T(8,128)(2,1)}, bf16[64,2048]{1,0:T(8,128)(2,1)}, bf16...) custom-call(bf16[256,2048]{1,0:T(8,128)(2,1)} %wide.1, bf16[128,2048]{1,0:T(8,128)(2,1)} %mid.1, bf16[64,2048]{1,0:T(8,128)(2,1)} %narrow.1, ...), custom_call_target="tpu_custom_call" | custom-call | flops 12000000000 | bytes 14680064 | tf_op jit(solution)/shard_map/pallas_call | solution.py:659
  78.7 5.8 %shard_map.242 = (bf16[512,512]{1,0:T(8,128)(2,1)}, bf16[256,2048]{1,0:T(8,128)(2,1)}, bf16[128,2048]{1,0:T(8,128)(2,1)}, bf16[64,2048]{1,0:T(8,128)(2,1)}, bf16...) custom-call(bf16[512,512]{1,0:T(8,128)(2,1)} %get-tuple-element.24.r, ...), custom_call_target="tpu_custom_call" | custom-call | tf_op jit(solution)/shard_map/pallas_call | solution.py:677

commit v3 on v2

--- a/solution.py
+++ b/solution.py
@@ -552,13 +552,6 @@
     ar_stage0(1)
     embed_grad(HALF)
     ar_stage1(0)
-
-    own_c[...] = dot(xm[...], ge[...], TN)
-    own_c[480:488] = jnp.concatenate(
-        [jnp.sum(v, axis=0, keepdims=True) for v in (*sums1, *sums2)] + [jnp.zeros((2, CH), F32)], axis=0
-    )
-    xs_c[...] = own_c[pl.ds(pl.multiple_of(other * 256, 256), 256)].astype(BF16)
-    core_copy(2).start()
 
     rg = dot(ge[...], pext[...], NT)
     first = jnp.where(eb == 0.0, rg[:, 0:128], jnp.where(eb == 1.0, rg[:, 256:384], rg[:, 384:512]))
@@ -598,7 +591,16 @@
             c.start()
             pending.append(c.wait)
 
-    lax.fori_loop(1, NDEV, send_grad, 0)
+    for k in range(1, NDEV):
+        send_grad(k, 0)
+
+    own_c[...] = dot(xm[...], ge[...], TN)
+    own_c[480:488] = jnp.concatenate(
+        [jnp.sum(v, axis=0, keepdims=True) for v in (*sums1, *sums2)] + [jnp.zeros((2, CH), F32)], axis=0
+    )
+    xs_c[...] = own_c[pl.ds(pl.multiple_of(other * 256, 256), 256)].astype(BF16)
+    core_copy(2).start()
+
     ar_stage2(0)
     ar_stage0(2)
     ar_stage1(1)

time: 84.8 us -> 84.3 us (level)
  no operation moved by 1% of the time
where the time goes in v3:
time: 84.3 us; the launch traced here: 84.1 us
  Pallas kernels  83.3 us (99%)
    pallas_call x1, Pallas kernels, shards(): pl.pallas_call(kernel, out_shape=[sds((LEN, CH), BF16), sds((256, ROWS),...  77.5 us
    pallas_call x1, Pallas kernels, shards(): pl.pallas_call(finish_kernel, out_shape=[sds(v.shape, v.dtype) for v in c...  5.75 us

profile of v3, /device:TPU:1, one launch (start us, length us, event | category | flops | bytes accessed | tf_op | source)
XLA Modules:
  0.0 84.1 jit_solution(15477818813551256823)
XLA Ops:
  0.6 77.5 %shard_map.241 = (bf16[512,512]{1,0:T(8,128)(2,1)}, bf16[256,2048]{1,0:T(8,128)(2,1)}, bf16[128,2048]{1,0:T(8,128)(2,1)}, bf16[64,2048]{1,0:T(8,128)(2,1)}, bf16...) custom-call(bf16[256,2048]{1,0:T(8,128)(2,1)} %wide.1, bf16[128,2048]{1,0:T(8,128)(2,1)} %mid.1, bf16[64,2048]{1,0:T(8,128)(2,1)} %narrow.1, ...), custom_call_target="tpu_custom_call" | custom-call | flops 12000000000 | bytes 14680064 | tf_op jit(solution)/shard_map/pallas_call | solution.py:661
  78.2 5.8 %shard_map.242 = (bf16[512,512]{1,0:T(8,128)(2,1)}, bf16[256,2048]{1,0:T(8,128)(2,1)}, bf16[128,2048]{1,0:T(8,128)(2,1)}, bf16[64,2048]{1,0:T(8,128)(2,1)}, bf16...) custom-call(bf16[512,512]{1,0:T(8,128)(2,1)} %get-tuple-element.24.r, ...), custom_call_target="tpu_custom_call" | custom-call | tf_op jit(solution)/shard_map/pallas_call | solution.py:679
